TPU v7x, 256 devices: a whole 4x4x8 slice. The times are simulated.
256 devices in a mesh: dp: 4 (over y), expert: 64 (over z, x, core).
Axes of the slice: x: 4, y: 4, z: 8, core: 2. Of those that a mesh axis runs over, the one named last changes fastest.
Arguments:
- tokens: bfloat16 [16384, 4096], P(('dp', 'expert')), may hold values from -6 to 6
- expert_ids: int32 [16384, 8], P(('dp', 'expert')), may hold values from 0 to 63, all different within a row; in each aligned block of 64 rows (0 to 63, 64 to 127, ...) at most 9 rows name the same one
- gate_values: float32 [16384, 8], P(('dp', 'expert')), may hold values from 0.05 to 0.5
- swap_mask: int32 [32], replicated, may hold values from 0 to 1, as said below
- gate_weight: bfloat16 [64, 4096, 1536], P('expert', None, 'dp'), may hold values from -0.09375 to 0.09375
- up_weight: bfloat16 [64, 4096, 1536], P('expert', None, 'dp'), may hold values from -0.09375 to 0.09375
- down_weight: bfloat16 [64, 1536, 4096], P('expert', 'dp'), may hold values from -0.15625 to 0.15625
Outputs:
- mixed: bfloat16 [16384, 4096], P(('dp', 'expert'))
Inputs may be any that keep to these rules, and one draw needn't show every extreme that they name: `expert_ids`: within each aligned block of 64 tokens (the tokens of one device) no slot is chosen more than 9 times, and some slot is chosen exactly 9 times in some block. A token's 8 slots differ. `swap_mask`: at least one pair exchanges and at least one pair does not.
All inputs are finite; a program needn't handle non-finite values.
Results may differ from a plain program's by a relative error of at most 0.015.
Values may be sent and summed in bfloat16 or wider, within the bound.
No kernel may reach another device: no remote copies, remote signals or barrier semaphores. Data moves between devices by JAX's collectives and lax.ppermute only.
A program may use at most 128 MiB of HBM per device.

v0:
```python
import functools
import jax
import jax.numpy as jnp
from jax import lax
from jax.experimental import pallas as pl
from jax.experimental.pallas import tpu as pltpu
from jax.sharding import Mesh, PartitionSpec as P

Y, Z, X, C = "y", "z", "x", "c"
ALL = (Y, Z, X, C)
XC = (X, C)
N_Y, N_Z, N_XC = 4, 8, 8
EXTRA = 128
VMEM = 20 << 20
VMEM_FFN = 52 << 20
FREE = pl.CostEstimate(flops=0, bytes_accessed=0, transcendentals=0)


def shift(block, axis, by):
    count = lax.axis_size(axis)
    return lax.ppermute(block, axis, [(i, (i + by) % count) for i in range(count)])


def after(value, *others):
    return lax.optimization_barrier((value, *others))[0]


def codes_kernel(mask_ref, tokens_ref, own_ref, other_ref, out_ref):
    count, width = tokens_ref.shape
    top = own_ref.shape[0] // 2
    experts = N_Z * N_XC
    slot = lax.broadcasted_iota(jnp.int32, (count, experts), 1)
    own = lax.broadcasted_iota(jnp.int32, (1, experts), 1)
    mask = jnp.concatenate([mask_ref[...], mask_ref[...]], axis=1)
    holder = jnp.where(mask == 1, own ^ (experts // 2), own).astype(jnp.float32)
    row = lax.broadcasted_iota(jnp.int32, (count, count), 0)
    earlier = (lax.broadcasted_iota(jnp.int32, (count, count), 1) < row).astype(jnp.bfloat16)
    lane = lax.broadcasted_iota(jnp.int32, (count, EXTRA), 1)
    out = jnp.zeros((count, EXTRA), jnp.float32)
    for ref, first in ((own_ref, 0), (other_ref, EXTRA // 2)):
        pairs = ref[...].T
        ids = pairs[:, :top].astype(jnp.int32)
        hits = [(ids[:, k : k + 1] == slot).astype(jnp.float32) for k in range(top)]
        chosen = functools.reduce(lambda p, q: p + q, hits)
        before = dot(earlier, chosen.astype(jnp.bfloat16))
        for k in range(top):
            out = jnp.where(lane == first + k, jnp.sum(hits[k] * holder, axis=1, keepdims=True), out)
            out = jnp.where(lane == first + top + k, jnp.sum(hits[k] * before, axis=1, keepdims=True), out)
            out = jnp.where(lane == first + 2 * top + k, pairs[:, top + k : top + k + 1], out)
    out_ref[:, :width] = tokens_ref[...]
    out_ref[:, width:] = out.astype(out_ref.dtype)


def with_codes(mask, tokens, own, other):
    return pl.pallas_call(
        codes_kernel,
        out_shape=jax.ShapeDtypeStruct((tokens.shape[0], tokens.shape[1] + EXTRA), jnp.bfloat16),
        cost_estimate=FREE,
    )(mask[None], tokens, own, other)


def rows_of(held_by, rank, token, per_z, capacity, z):
    held_by = held_by.astype(jnp.int32)
    row = ((held_by & (N_XC - 1)) * N_Z + token // per_z) * capacity + rank.astype(jnp.int32)
    return jnp.where(held_by // N_XC == z, row, -1)


def picks_kernel(first, top, capacity, z_ref, extra_ref, out_ref):
    across = extra_ref[...].astype(jnp.float32).T[first : first + 2 * top]
    count = across.shape[1]
    token = lax.broadcasted_iota(jnp.int32, (top, count), 1)
    row = rows_of(across[:top], across[top:], token, count // N_Z, capacity, z_ref[0])
    slot = lax.broadcasted_iota(jnp.int32, out_ref.shape, 0)
    hit = jnp.zeros(out_ref.shape, jnp.float32)
    for k in range(top):
        hit = jnp.where(row[k : k + 1] == slot, 1.0, hit)
    out_ref[...] = hit.astype(out_ref.dtype)


def mixes_kernel(first, top, capacity, z_ref, extra_ref, out_ref):
    values = extra_ref[:, first : first + 3 * top].astype(jnp.float32)
    count = values.shape[0]
    token = lax.broadcasted_iota(jnp.int32, (count, top), 0)
    row = rows_of(values[:, :top], values[:, top : 2 * top], token, count // N_Z, capacity, z_ref[0])
    slot = lax.broadcasted_iota(jnp.int32, out_ref.shape, 1)
    total = jnp.zeros(out_ref.shape, jnp.float32)
    for k in range(top):
        total = jnp.where(row[:, k : k + 1] == slot, values[:, 2 * top + k : 2 * top + k + 1], total)
    out_ref[...] = total.astype(out_ref.dtype)


def matrix(kernel, gathered, first, top, capacity, shape):
    count, width = gathered.shape
    return pl.pallas_call(
        functools.partial(kernel, first, top, capacity),
        grid=(1,),
        in_specs=[
            pl.BlockSpec(memory_space=pltpu.SMEM),
            pl.BlockSpec((count, EXTRA), lambda j: (0, width // EXTRA - 1)),
        ],
        out_specs=pl.BlockSpec(shape, lambda j: (0, 0)),
        out_shape=jax.ShapeDtypeStruct(shape, jnp.bfloat16),
        compiler_params=pltpu.CompilerParams(vmem_limit_bytes=VMEM),
        cost_estimate=FREE,
    )(lax.axis_index(Z).astype(jnp.int32)[None], gathered)


def apply_kernel(matrix_ref, value_ref, out_ref):
    out_ref[...] = dot(matrix_ref[...], value_ref[...]).astype(out_ref.dtype)


def apply(matrix, value, first, width, tile):
    rows, inner = matrix.shape
    at = first // tile
    return pl.pallas_call(
        apply_kernel,
        grid=(width // tile,),
        in_specs=[pl.BlockSpec((rows, inner), lambda j: (0, 0)), pl.BlockSpec((inner, tile), lambda j: (0, j + at))],
        out_specs=pl.BlockSpec((rows, tile), lambda j: (0, j)),
        out_shape=jax.ShapeDtypeStruct((rows, width), jnp.bfloat16),
        compiler_params=pltpu.CompilerParams(vmem_limit_bytes=VMEM),
        cost_estimate=FREE,
    )(matrix, value)


def sides_kernel(bounds, gate_ref, up_ref, *out_refs):
    units = gate_ref.shape[1]
    third, half = units // 3, units // 2
    gate, up = gate_ref[...], up_ref[...]
    low = jnp.concatenate([gate[:, :third], up[:, :third], gate[:, third:half], up[:, third:half]], axis=1)
    high = jnp.concatenate(
        [gate[:, units - third :], up[:, units - third :], gate[:, half : units - third], up[:, half : units - third]], axis=1
    )
    step = pl.program_id(0)
    for i, (first, last) in enumerate(zip(bounds, bounds[1:])):

        @pl.when((step >= first) & (step < last))
        def _():
            out_refs[2 * i][...] = low
            out_refs[2 * i + 1][...] = high


def sides(gate, up, bounds, tile):
    rows, units = gate.shape
    steps = [bound // tile for bound in bounds]

    def spec(first, last):
        return pl.BlockSpec((tile, units), lambda j: (jnp.clip(j - first, 0, last - first - 1), 0))

    ranges = [r for r in zip(bounds, bounds[1:]) for _ in range(2)]
    outs = pl.pallas_call(
        functools.partial(sides_kernel, steps),
        grid=(rows // tile,),
        in_specs=[pl.BlockSpec((tile, units), lambda j: (j, 0))] * 2,
        out_specs=[spec(first // tile, last // tile) for first, last in ranges],
        out_shape=[jax.ShapeDtypeStruct((last - first, units), gate.dtype) for first, last in ranges],
        compiler_params=pltpu.CompilerParams(vmem_limit_bytes=VMEM),
        cost_estimate=FREE,
    )(gate, up)
    return list(zip(outs[::2], outs[1::2]))


def ffn_kernel(moves, has_add, rows_ref, gate_ref, up_ref, *refs):
    side_refs, act_ref = refs[:6], refs[6]
    out_ref, low_ref, high_ref, weights, sems = refs[6 + has_add :]
    step = pl.program_id(0)
    third = gate_ref.shape[1]
    sixth = third // 2
    first_two = 2 * third
    copies = [
        pltpu.make_async_copy(
            side_refs[2 * i + j].at[pl.ds(source, count)], buffer.at[pl.ds(target, count)], sems.at[2 * i + j]
        )
        for i, source, target, count in moves
        for j, buffer in enumerate((low_ref, high_ref))
    ]

    @pl.when(step == 0)
    def _():
        for copy in copies:
            copy.start()

    @pl.when(step < 3)
    def _():
        weights[:, :third] = gate_ref[...]
        weights[:, third:] = up_ref[...]

    @pl.when(step == 3)
    def _():
        for copy in copies:
            copy.wait()
        weights[...] = low_ref[:, :first_two]

    @pl.when(step == 4)
    def _():
        low, high = low_ref[:, first_two:], high_ref[:, first_two:]
        weights[...] = jnp.concatenate([low[:, :sixth], high[:, :sixth], low[:, sixth:], high[:, sixth:]], axis=1)

    @pl.when(step == 5)
    def _():
        weights[...] = high_ref[:, :first_two]

    act = dot(rows_ref[...], weights[...])
    if has_add:
        act = act + act_ref[...]
        act = jax.nn.silu(act[:, :third]) * act[:, third:]
    out_ref[...] = act.astype(out_ref.dtype)


def ffn(rows, first, gate, up, side_weights, bounds, act=None):
    count, inner = rows.shape
    units = gate.shape[1]
    third = units // 3
    last = first + inner
    moves = []
    for i, (low, high) in enumerate(zip(bounds, bounds[1:])):
        start, stop = max(low, first), min(high, last)
        if start < stop:
            moves.append((i, start - low, start - first, stop - start))
    has_add = act is not None
    columns, dtype = (third, jnp.bfloat16) if has_add else (2 * third, jnp.float32)
    weight = pl.BlockSpec((inner, third), lambda j: (first // inner, jnp.minimum(j, 2)))
    return pl.pallas_call(
        functools.partial(ffn_kernel, moves, has_add),
        grid=(6,),
        in_specs=[pl.BlockSpec((count, inner), lambda j: (0, 0)), weight, weight]
        + [pl.BlockSpec(memory_space=pltpu.HBM)] * 6
        + [pl.BlockSpec((count, 2 * third), lambda j: (0, j))] * has_add,
        out_specs=pl.BlockSpec((count, columns), lambda j: (0, j)),
        out_shape=jax.ShapeDtypeStruct((count, 6 * columns), dtype),
        scratch_shapes=[
            pltpu.VMEM((inner, units), gate.dtype),
            pltpu.VMEM((inner, units), gate.dtype),
            pltpu.VMEM((inner, 2 * third), gate.dtype),
            pltpu.SemaphoreType.DMA((6,)),
        ],
        compiler_params=pltpu.CompilerParams(vmem_limit_bytes=VMEM_FFN),
        cost_estimate=pl.CostEstimate(flops=12 * count * inner * units, bytes_accessed=6 * inner * units, transcendentals=0),
    )(rows, gate, up, *side_weights, *([act] if has_add else []))


def down_kernel(has_add, hidden_ref, own_ref, low_ref, high_ref, *refs):
    weights = jnp.concatenate([own_ref[...], low_ref[...], high_ref[...]], axis=0)
    result = dot(hidden_ref[...], weights)
    if has_add:
        result = result + refs[0][...].astype(jnp.float32)
    refs[-1][...] = result.astype(refs[-1].dtype)


def down(hidden, own, low, high, first, width, tile, add=None):
    count, units = hidden.shape
    at = first // tile
    half = low.shape[0]
    extra = [] if add is None else [add]
    return pl.pallas_call(
        functools.partial(down_kernel, add is not None),
        grid=(width // tile,),
        in_specs=[
            pl.BlockSpec((count, units), lambda j: (0, 0)),
            pl.BlockSpec((own.shape[0], tile), lambda j: (0, j + at)),
            pl.BlockSpec((half, tile), lambda j: (0, j + at)),
            pl.BlockSpec((half, tile), lambda j: (0, j + at)),
        ]
        + [pl.BlockSpec((count, tile), lambda j: (0, j))] * len(extra),
        out_specs=pl.BlockSpec((count, tile), lambda j: (0, j)),
        out_shape=jax.ShapeDtypeStruct((count, width), jnp.bfloat16),
        compiler_params=pltpu.CompilerParams(vmem_limit_bytes=VMEM),
        cost_estimate=FREE,
    )(hidden, own, low, high, *extra)


def dot(a, b):
    return jnp.dot(a, b, preferred_element_type=jnp.float32)


def exchange(rows):
    parts = rows.reshape(N_XC, rows.shape[0] // N_XC, rows.shape[1])
    return lax.all_to_all(parts, XC, split_axis=0, concat_axis=0, tiled=True).reshape(rows.shape)


def local(tokens, expert_ids, gate_values, swap_mask, gate_weight, up_weight, down_weight):
    tok_count, width = tokens.shape
    top = expert_ids.shape[1]
    experts = N_Z * N_XC
    capacity = min(tok_count, tok_count * top // experts + 1)
    cut = width // 2
    tile = min(512, cut)
    back = width // 8 * 5
    rest = width - back
    w_gate, w_up, w_down = gate_weight[0], up_weight[0], down_weight[0]
    units = w_gate.shape[1]
    half = units // 2

    pairs = jnp.concatenate([expert_ids.T.astype(jnp.float32), gate_values.T], axis=0)
    down_parts = after((w_down[:half], w_down[half:]), pairs)
    pairs_other, *down_parts = lax.optimization_barrier((shift(pairs, Y, 2), *down_parts))
    own_tokens = with_codes(swap_mask, tokens, pairs, pairs_other)
    other_tokens = shift(after(tokens[:, :cut], own_tokens), Y, 2)

    def swap(parts):
        return shift(parts[0], Y, -1), shift(parts[1], Y, 1)

    bounds = [0, width // 16 * 6, width // 16 * 11, width]
    side_2, side_1, side_0 = sides(after(w_gate, own_tokens), w_up, bounds, width // 16)
    down_low, down_high = swap(down_parts)
    side_0 = swap(after(side_0, down_low, down_high, other_tokens))
    side_1 = swap(after(side_1, *side_0))
    side_2 = swap(after(side_2, *side_1))

    own_all = lax.all_gather(own_tokens, Z, axis=0, tiled=True)
    other_all = lax.all_gather(after(other_tokens, own_tokens), Z, axis=0, tiled=True)
    own_all = after(own_all, down_low, down_high)

    late_width = width - cut
    rows, count = N_XC * N_Z * capacity, N_Z * tok_count
    second = EXTRA // 2
    pick_own = matrix(picks_kernel, own_all, 0, top, capacity, (rows, count))
    late_rows = apply(pick_own, own_all, cut, late_width, tile)
    own_rows = apply(after(pick_own, late_rows), own_all, 0, cut, tile)
    own_late = exchange(after(late_rows, own_rows, *side_0))
    own_early = exchange(after(own_rows, own_late, *side_1))
    mix_own = matrix(mixes_kernel, after(own_all, own_rows), 0, top, capacity, (count, rows))
    pick_other = matrix(picks_kernel, after(own_all, mix_own), second, top, capacity, (rows, count))
    other_rows = apply(pick_other, other_all, 0, cut, tile)
    other_early = exchange(after(other_rows, own_early, *side_2))
    mix_other = matrix(mixes_kernel, after(own_all, other_rows), second, top, capacity, (count, rows))
    other_late = shift(after(own_late, *side_2), Y, 2)

    side_weights = (*side_2, *side_1, *side_0)

    def part(rows, first, act=None):
        return ffn(rows, first, w_gate, w_up, side_weights, bounds, act)

    early_down = (w_down, down_low, down_high, 0, back, tile)
    late_down = (w_down, down_low, down_high, back, rest, tile)
    hidden_own = part(own_early, 0, part(own_late, cut))
    own_out = down(hidden_own, *early_down)
    own_back = exchange(after(own_out, other_early))
    hidden_other = part(other_late, cut, part(other_early, 0))
    late_for_other = down(hidden_other, *late_down)
    late_from_other = shift(late_for_other, Y, 2)
    other_out = down(after(hidden_other, late_for_other), *early_down)

    own_mixed = apply(mix_own, after(own_back, other_out), 0, back, tile)
    own_sum = lax.psum_scatter(own_mixed, Z, scatter_dimension=0, tiled=True)
    other_back = exchange(other_out)
    other_mixed = apply(mix_other, other_back, 0, back, tile)
    other_sum = lax.psum_scatter(after(other_mixed, late_from_other, own_sum), Z, scatter_dimension=0, tiled=True)
    early_final = own_sum.astype(jnp.float32) + shift(other_sum, Y, 2).astype(jnp.float32)

    late_out = down(hidden_own, *late_down, late_from_other)
    late_back = exchange(after(late_out, other_mixed))
    late_final = lax.psum_scatter(apply(mix_own, late_back, 0, rest, tile), Z, scatter_dimension=0, tiled=True)
    result = jnp.pad(early_final.astype(jnp.bfloat16), ((0, 0), (0, rest)))
    return lax.dynamic_update_slice(result, late_final, (0, back))


def solution(mesh):
    fine = Mesh(mesh.devices.reshape(N_Y, N_Z, N_XC // 2, 2), ALL)
    experts = (Z, X, C)
    placed = (
        P(ALL, None),
        P(ALL, None),
        P(ALL, None),
        P(),
        P(experts, None, Y),
        P(experts, None, Y),
        P(experts, Y, None),
    )
    return jax.shard_map(local, mesh=fine, in_specs=placed, out_specs=P(ALL, None), check_vma=False)
```

profile of v0, /device:TPU:4, one launch (start us, length us, event | category | flops | bytes accessed | tf_op | source)
XLA Modules:
  0.0 384.3 jit_solution(5883031864802193127)
XLA Ops:
  7.9 3.2 collective-permute-start
  11.1 3.9 %slice_bitcast_fusion = (bf16[192,4096]{1,0:T(8,128)(2,1)}, bf16[192,4096]{1,0:T(8,128)(2,1)}) fusion(bf16[1,384,4096]{2,1,0:T(8,128)(2,1)} %param.13), kind=kLoop, calls=%fused_computation | loop fusion | bytes 6291456 | tf_op jit(solution)/shard_map/slice | solution.py:295
  15.7 3.2 shard_map.73
  21.9 1.3 collective-permute-start.3
  23.2 1.9 copy-done.23
  25.1 1.9 copy-done.24
  27.0 2.4 shard_map.78
  35.3 26.1 %collective-permute-done.3 = bf16[64,2048]{1,0:T(8,128)(2,1)S(1)} collective-permute-done((bf16[64,2048]{1,0:T(8,128)(2,1)S(1)}, bf16[64,2048]{1,0:T(8,128)(2,1)S(1)}, u32[]{:S(2)}, u32[]{:S(2)}) %collective-permute-start.3) | collective-permute-done | bytes 262176 | tf_op jit(solution)/shard_map/ppermute | solution.py:21
  61.5 1.1 collective-permute-done.2.high_ref
  63.4 1.2 collective-permute-start.5
  64.6 11.4 %all-gather.3.cloned.1.call-done.extra_ref.value_ref = bf16[512,4224]{1,0:T(8,128)(2,1)} async-done(((bf16[64,4224]{1,0:T(8,128)(2,1)}), bf16[512,4224]{1,0:T(8,128)(2,1)}) %all-gather.3.cloned.1.call-update) | async-done | bytes 4325392 | tf_op jit(solution)/shard_map/all_gather | solution.py:310
  76.1 2.2 copy-done
  78.3 1.8 shard_map.74.matrix_ref
  80.5 2.3 shard_map.75
  82.8 1.5 copy-done.17
  84.3 3.3 shard_map.76
  87.6 4.9 %all-to-all-start = ((bf16[8,72,2048]{2,1,0:T(8,128)(2,1)}), bf16[8,72,2048]{2,1,0:T(8,128)(2,1)}, u32[]{:S(2)}, u32[]{:S(2)}) async-start(bf16[8,72,2048]{2,1,0:T(8,128)(2,1)} %bitcast.30), calls=%async_computation | async-start | bytes 4718592 | tf_op jit(solution)/shard_map/all_to_all | solution.py:278
  93.3 2.8 collective-permute-start.6
  96.1 21.3 %collective-permute-done.6.refs_2_ = bf16[1280,384]{1,0:T(8,128)(2,1)S(1)} collective-permute-done((bf16[1280,384]{1,0:T(8,128)(2,1)S(1)}, bf16[1280,384]{1,0:T(8,128)(2,1)S(1)}, u32[]{:S(2)}, u32[]{:S(2)}) %collective-permute-start.6) | collective-permute-done | bytes 983072 | tf_op jit(solution)/shard_map/ppermute | solution.py:21
  118.4 2.5 collective-permute-done.7.refs_3_
  121.9 5.2 %all-to-all-start.1 = ((bf16[8,72,2048]{2,1,0:T(8,128)(2,1)}), bf16[8,72,2048]{2,1,0:T(8,128)(2,1)}, u32[]{:S(2)}, u32[]{:S(2)}) async-start(bf16[8,72,2048]{2,1,0:T(8,128)(2,1)} %bitcast.10), calls=%async_computation.1 | async-start | bytes 4718592 | tf_op jit(solution)/shard_map/all_to_all | solution.py:278
  127.1 2.7 collective-permute-start.8
  129.8 2.2 copy-done.2
  132.1 2.3 shard_map.77.matrix_ref
  135.2 1.8 shard_map.82.matrix_ref
  137.1 1.6 copy-done.27
  138.7 3.3 shard_map.83
  142.0 13.4 %collective-permute-done.8.refs_0_ = bf16[1536,384]{1,0:T(8,128)(2,1)} collective-permute-done((bf16[1536,384]{1,0:T(8,128)(2,1)S(1)}, bf16[1536,384]{1,0:T(8,128)(2,1)}, u32[]{:S(2)}, u32[]{:S(2)}) %collective-permute-start.8) | collective-permute-done | bytes 1179680 | tf_op jit(solution)/shard_map/ppermute | solution.py:21
  155.4 3.5 collective-permute-done.9.refs_1_
  158.9 4.9 %all-to-all-start.2 = ((bf16[8,72,2048]{2,1,0:T(8,128)(2,1)}), bf16[8,72,2048]{2,1,0:T(8,128)(2,1)}, u32[]{:S(2)}, u32[]{:S(2)}) async-start(bf16[8,72,2048]{2,1,0:T(8,128)(2,1)} %bitcast.13), calls=%async_computation.2 | async-start | bytes 4718592 | tf_op jit(solution)/shard_map/all_to_all | solution.py:278
  164.7 9.7 %shard_map.79.refs_6_ = f32[576,1536]{1,0:T(8,128)} custom-call(bf16[576,2048]{1,0:T(8,128)(2,1)} %bitcast.9.rows_ref, bf16[4096,384]{1,0:T(8,128)(2,1)} %bitcast.33, bf16[4096,384]{1,0:T(8,128)(2,1)} %bitcast.38, bf16[1536,384]{1,0:T(8,128)(2,1)} %collective-permute-done.8.refs_0_, bf16[1536,384]{1,0:T(8,128)(2,1)} %collective-permute-done.9.refs_1_, ...), custom_call_target="tpu_custom_call" | custom-call | flops 5435817984 | bytes 4718592 | tf_op jit(solution)/shard_map/pallas_call | solution.py:223
  174.4 10.1 %shard_map.80.hidden_ref = bf16[576,768]{1,0:T(8,128)(2,1)S(1)} custom-call(bf16[576,2048]{1,0:T(8,128)(2,1)} %bitcast.11.rows_ref, bf16[4096,384]{1,0:T(8,128)(2,1)} %bitcast.34, bf16[4096,384]{1,0:T(8,128)(2,1)} %bitcast.39, bf16[1536,384]{1,0:T(8,128)(2,1)} %collective-permute-done.8.refs_0_, bf16[1536,384]{1,0:T(8,128)(2,1)} %collective-permute-done.9.refs_1_, ...), custom_call_target="tpu_custom_call" | custom-call | flops 5435817984 | bytes 4718592 | tf_op jit(solution)/shard_map/pallas_call | solution.py:223
  184.5 3.6 shard_map.81
  188.1 1.6 copy-done.13
  190.8 7.5 %all-to-all-start.3 = ((bf16[8,72,2560]{2,1,0:T(8,128)(2,1)}), bf16[8,72,2560]{2,1,0:T(8,128)(2,1)}, u32[]{:S(2)}, u32[]{:S(2)}) async-start(bf16[8,72,2560]{2,1,0:T(8,128)(2,1)} %bitcast.28), calls=%async_computation.3 | async-start | bytes 5898240 | tf_op jit(solution)/shard_map/all_to_all | solution.py:278
  198.3 1.2 copy-done.36
  199.5 1.2 copy-done.40
  200.7 9.8 %shard_map.84.refs_6_ = f32[576,1536]{1,0:T(8,128)} custom-call(bf16[576,2048]{1,0:T(8,128)(2,1)} %bitcast.14.rows_ref, bf16[4096,384]{1,0:T(8,128)(2,1)} %bitcast.35, bf16[4096,384]{1,0:T(8,128)(2,1)} %bitcast.40, bf16[1536,384]{1,0:T(8,128)(2,1)} %collective-permute-done.8.refs_0_, bf16[1536,384]{1,0:T(8,128)(2,1)} %collective-permute-done.9.refs_1_, ...), custom_call_target="tpu_custom_call" | custom-call | flops 5435817984 | bytes 4718592 | tf_op jit(solution)/shard_map/pallas_call | solution.py:223
  210.5 8.4 %collective-permute-done.10.rows_ref = bf16[576,2048]{1,0:T(8,128)(2,1)} collective-permute-done((bf16[576,2048]{1,0:T(8,128)(2,1)}, bf16[576,2048]{1,0:T(8,128)(2,1)}, u32[]{:S(2)}, u32[]{:S(2)}) %collective-permute-start.10) | collective-permute-done | bytes 2359328 | tf_op jit(solution)/shard_map/ppermute | solution.py:21
  219.0 9.3 %shard_map.85.hidden_ref = bf16[576,768]{1,0:T(8,128)(2,1)S(1)} custom-call(bf16[576,2048]{1,0:T(8,128)(2,1)} %collective-permute-done.10.rows_ref, bf16[4096,384]{1,0:T(8,128)(2,1)} %bitcast.36, bf16[4096,384]{1,0:T(8,128)(2,1)} %bitcast.41, bf16[1536,384]{1,0:T(8,128)(2,1)} %collective-permute-done.8.refs_0_, ...), custom_call_target="tpu_custom_call" | custom-call | flops 5435817984 | bytes 4718592 | tf_op jit(solution)/shard_map/pallas_call | solution.py:223
  228.3 2.2 shard_map.86
  230.5 1.2 copy-done.28
  231.7 3.6 shard_map.87
  235.3 1.6 copy-done.14
  238.0 5.0 %shard_map.88 = bf16[512,2560]{1,0:T(8,128)(2,1)S(1)} custom-call(bf16[512,576]{1,0:T(8,128)(2,1)S(1)} %copy-done.19, bf16[576,2560]{1,0:T(8,128)(2,1)} %bitcast.16.value_ref), custom_call_target="tpu_custom_call" | custom-call | tf_op jit(solution)/shard_map/pallas_call | solution.py:115
  243.0 1.6 copy-done.16
  244.6 4.8 %all-to-all-start.4 = ((bf16[8,72,2560]{2,1,0:T(8,128)(2,1)}), bf16[8,72,2560]{2,1,0:T(8,128)(2,1)}, u32[]{:S(2)}, u32[]{:S(2)}) async-start(bf16[8,72,2560]{2,1,0:T(8,128)(2,1)} %bitcast.29), calls=%async_computation.5 | async-start | bytes 5898240 | tf_op jit(solution)/shard_map/all_to_all | solution.py:278
  250.3 2.2 copy-done.3
  252.5 2.3 shard_map.89.matrix_ref
  255.6 27.1 %all-to-all-done.4 = bf16[8,72,2560]{2,1,0:T(8,128)(2,1)} async-done(((bf16[8,72,2560]{2,1,0:T(8,128)(2,1)}), bf16[8,72,2560]{2,1,0:T(8,128)(2,1)}, u32[]{:S(2)}, u32[]{:S(2)}) %all-to-all-start.4) | async-done | bytes 2949152 | tf_op jit(solution)/shard_map/all_to_all | solution.py:278
  283.8 5.0 %shard_map.90 = bf16[512,2560]{1,0:T(8,128)(2,1)S(1)} custom-call(bf16[512,576]{1,0:T(8,128)(2,1)S(1)} %copy-done.26, bf16[576,2560]{1,0:T(8,128)(2,1)} %bitcast.18.value_ref), custom_call_target="tpu_custom_call" | custom-call | tf_op jit(solution)/shard_map/pallas_call | solution.py:115
  288.9 1.5 copy-done.15
  290.3 1.6 collective-permute-done.11.refs_0_
  292.0 1.4 copy-done.8
  293.4 1.4 copy-done.12
  294.8 1.2 copy-done.22
  296.0 3.6 shard_map.91
  299.6 25.8 %all_to_all.30 = bf16[8,72,1536]{2,1,0:T(8,128)(2,1)S(1)} all-to-all(bf16[8,72,1536]{2,1,0:T(8,128)(2,1)S(1)} %bitcast.32), channel_id=1, replica_groups=mesh['y'=4,'z'=8,'x'=4,'c'=2] {'x','c'}, dimensions={0} | all-to-all | bytes 3538944 | tf_op jit(solution)/shard_map/all_to_all | solution.py:278
  325.4 2.9 shard_map.92
  328.3 5.5 %reduce-scatter.6.cloned.1.call-done = bf16[64,2560]{1,0:T(8,128)(2,1)} async-done(((bf16[512,2560]{1,0:T(8,128)(2,1)}), bf16[64,2560]{1,0:T(8,128)(2,1)}) %reduce-scatter.6.cloned.1.call-update) | async-done | bytes 327696 | tf_op jit(solution)/shard_map/reduce_scatter | solution.py:348
  333.7 2.8 collective-permute-start.12
  336.6 6.0 %collective-permute-done.12 = bf16[64,2560]{1,0:T(8,128)(2,1)S(1)} collective-permute-done((bf16[64,2560]{1,0:T(8,128)(2,1)}, bf16[64,2560]{1,0:T(8,128)(2,1)S(1)}, u32[]{:S(2)}, u32[]{:S(2)}) %collective-permute-start.12) | collective-permute-done | bytes 327712 | tf_op jit(solution)/shard_map/ppermute | solution.py:21
  342.6 33.4 %reduce-scatter.8.cloned.1.call-done = bf16[64,1536]{1,0:T(8,128)(2,1)} async-done(((bf16[512,1536]{1,0:T(8,128)(2,1)}), bf16[64,1536]{1,0:T(8,128)(2,1)}) %reduce-scatter.8.cloned.1.call-update) | async-done | bytes 196624 | tf_op jit(solution)/shard_map/reduce_scatter | solution.py:353
  376.0 1.8 pad_maximum_fusion
  (116 shorter events, 21.8 us)
Async XLA Ops:
  6.5 69.5 %all-gather.3.cloned.1.call-start = ((), (), s32[]{:S(2)}) async-start(), calls=%async_computation.9 | async-start | bytes 4866048 | tf_op jit(solution)/shard_map/all_gather | solution.py:310
  7.9 7.1 %copy-start.49 = (f32[16,64]{1,0:T(8,128)}, f32[16,64]{1,0:T(8,128)S(1)}, u32[]{:S(2)}) copy-start(f32[16,64]{1,0:T(8,128)S(1)} %pad_maximum_fusion.1.own_ref) | copy-start | bytes 12292
  7.9 7.1 %collective-permute-start = (f32[16,64]{1,0:T(8,128)S(1)}, f32[16,64]{1,0:T(8,128)S(1)}, u32[]{:S(2)}, u32[]{:S(2)}) collective-permute-start(f32[16,64]{1,0:T(8,128)S(1)} %pad_maximum_fusion.1.own_ref), channel_id=1, source_target_pairs={{0,128},{64,192},{128,0},{192,64},{1,129},{65,193},{129,1},{193,65... | collective-permute-start | bytes 12296 | tf_op jit(solution)/shard_map/ppermute | solution.py:21
  18.9 42.6 %collective-permute-start.1 = (bf16[192,4096]{1,0:T(8,128)(2,1)}, bf16[192,4096]{1,0:T(8,128)(2,1)S(1)}, u32[]{:S(2)}, u32[]{:S(2)}) collective-permute-start(bf16[192,4096]{1,0:T(8,128)(2,1)} %get-tuple-element.42), channel_id=1, source_target_pairs={{0,192},{64,0},{128,64},{192,128},{1,193},{65,1},{129,65},{193,129... | collective-permute-start | bytes 4718600 | tf_op jit(solution)/shard_map/ppermute | solution.py:21
  20.0 42.6 %collective-permute-start.2 = (bf16[192,4096]{1,0:T(8,128)(2,1)}, bf16[192,4096]{1,0:T(8,128)(2,1)S(1)}, u32[]{:S(2)}, u32[]{:S(2)}) collective-permute-start(bf16[192,4096]{1,0:T(8,128)(2,1)} %get-tuple-element.43), channel_id=1, source_target_pairs={{0,64},{64,128},{128,192},{192,0},{1,65},{65,129},{129,193},{193,1... | collective-permute-start | bytes 4718600 | tf_op jit(solution)/shard_map/ppermute | solution.py:21
  21.9 39.5 %collective-permute-start.3 = (bf16[64,2048]{1,0:T(8,128)(2,1)S(1)}, bf16[64,2048]{1,0:T(8,128)(2,1)S(1)}, u32[]{:S(2)}, u32[]{:S(2)}) collective-permute-start(bf16[64,2048]{1,0:T(8,128)(2,1)S(1)} %slice.19), channel_id=1, source_target_pairs={{0,128},{64,192},{128,0},{192,64},{1,129},{65,193},{129,1},{193,65... | collective-permute-start | bytes 786440 | tf_op jit(solution)/shard_map/ppermute | solution.py:21
  23.2 1.9 copy-start.23
  25.1 1.9 copy-start.24
  30.4 1.0 copy-start.31
  61.5 18.7 %copy-start.48 = (bf16[64,2048]{1,0:T(8,128)(2,1)}, bf16[64,2048]{1,0:T(8,128)(2,1)S(1)}, u32[]{:S(2)}) copy-start(bf16[64,2048]{1,0:T(8,128)(2,1)S(1)} %collective-permute-done.3) | copy-start | bytes 786436
  61.5 18.7 %copy-start.5 = (bf16[192,4096]{1,0:T(8,128)(2,1)}, bf16[192,4096]{1,0:T(8,128)(2,1)S(1)}, u32[]{:S(2)}) copy-start(bf16[192,4096]{1,0:T(8,128)(2,1)S(1)} %collective-permute-done.1.low_ref) | copy-start | bytes 4718596
  62.6 17.5 %copy-start.9 = (bf16[192,4096]{1,0:T(8,128)(2,1)}, bf16[192,4096]{1,0:T(8,128)(2,1)S(1)}, u32[]{:S(2)}) copy-start(bf16[192,4096]{1,0:T(8,128)(2,1)S(1)} %collective-permute-done.2.high_ref) | copy-start | bytes 4718596
  62.6 25.0 %collective-permute-start.4 = (bf16[1280,384]{1,0:T(8,128)(2,1)}, bf16[1280,384]{1,0:T(8,128)(2,1)}, u32[]{:S(2)}, u32[]{:S(2)}) collective-permute-start(bf16[1280,384]{1,0:T(8,128)(2,1)} %copy-done.46), channel_id=1, source_target_pairs={{0,192},{64,0},{128,64},{192,128},{1,193},{65,1},{129,65},{193,129... | collective-permute-start | bytes 2949128 | tf_op jit(solution)/shard_map/ppermute | solution.py:21
  63.4 24.2 %collective-permute-start.5 = (bf16[1280,384]{1,0:T(8,128)(2,1)}, bf16[1280,384]{1,0:T(8,128)(2,1)}, u32[]{:S(2)}, u32[]{:S(2)}) collective-permute-start(bf16[1280,384]{1,0:T(8,128)(2,1)} %copy-done.45), channel_id=1, source_target_pairs={{0,64},{64,128},{128,192},{192,0},{1,65},{65,129},{129,193},{193,1... | collective-permute-start | bytes 2949128 | tf_op jit(solution)/shard_map/ppermute | solution.py:21
  76.1 2.2 copy-start
  78.3 2.2 copy-start.1
  82.8 1.5 copy-start.17
  87.6 5.7 %copy-start.44 = (bf16[1280,384]{1,0:T(8,128)(2,1)S(1)}, bf16[1280,384]{1,0:T(8,128)(2,1)}, u32[]{:S(2)}) copy-start(bf16[1280,384]{1,0:T(8,128)(2,1)} %copy-done.43) | copy-start | bytes 2949124
  87.6 8.5 %copy-start.42 = (bf16[1280,384]{1,0:T(8,128)(2,1)S(1)}, bf16[1280,384]{1,0:T(8,128)(2,1)}, u32[]{:S(2)}) copy-start(bf16[1280,384]{1,0:T(8,128)(2,1)} %copy-done.41) | copy-start | bytes 2949124
  87.6 34.3 %all-to-all-start = ((bf16[8,72,2048]{2,1,0:T(8,128)(2,1)}), bf16[8,72,2048]{2,1,0:T(8,128)(2,1)}, u32[]{:S(2)}, u32[]{:S(2)}) async-start(bf16[8,72,2048]{2,1,0:T(8,128)(2,1)} %bitcast.30), calls=%async_computation | async-start | bytes 4718592 | tf_op jit(solution)/shard_map/all_to_all | solution.py:278
  92.6 44.5 %all-gather.5.cloned.1.call-start = ((), (), s32[]{:S(2)}) async-start(), calls=%async_computation.10 | async-start | bytes 2359296 | tf_op jit(solution)/shard_map/all_gather | solution.py:311
  93.3 24.1 %collective-permute-start.6 = (bf16[1280,384]{1,0:T(8,128)(2,1)S(1)}, bf16[1280,384]{1,0:T(8,128)(2,1)S(1)}, u32[]{:S(2)}, u32[]{:S(2)}) collective-permute-start(bf16[1280,384]{1,0:T(8,128)(2,1)S(1)} %copy-done.44), channel_id=1, source_target_pairs={{0,192},{64,0},{128,64},{192,128},{1,193},{65,1},{129,65},{193,129... | collective-permute-start | bytes 2949128 | tf_op jit(solution)/shard_map/ppermute | solution.py:21
  96.1 24.7 %collective-permute-start.7 = (bf16[1280,384]{1,0:T(8,128)(2,1)S(1)}, bf16[1280,384]{1,0:T(8,128)(2,1)S(1)}, u32[]{:S(2)}, u32[]{:S(2)}) collective-permute-start(bf16[1280,384]{1,0:T(8,128)(2,1)S(1)} %copy-done.42), channel_id=1, source_target_pairs={{0,64},{64,128},{128,192},{192,0},{1,65},{65,129},{129,193},{193,1... | collective-permute-start | bytes 2949128 | tf_op jit(solution)/shard_map/ppermute | solution.py:21
  120.9 1.0 copy-start.38
  121.9 5.2 %copy-start.32 = (bf16[1536,384]{1,0:T(8,128)(2,1)S(1)}, bf16[1536,384]{1,0:T(8,128)(2,1)}, u32[]{:S(2)}) copy-start(bf16[1536,384]{1,0:T(8,128)(2,1)} %copy-done.31) | copy-start | bytes 3538948
  121.9 7.9 %copy-start.30 = (bf16[1536,384]{1,0:T(8,128)(2,1)S(1)}, bf16[1536,384]{1,0:T(8,128)(2,1)}, u32[]{:S(2)}) copy-start(bf16[1536,384]{1,0:T(8,128)(2,1)} %copy-done.29) | copy-start | bytes 3538948
  121.9 37.0 %all-to-all-start.1 = ((bf16[8,72,2048]{2,1,0:T(8,128)(2,1)}), bf16[8,72,2048]{2,1,0:T(8,128)(2,1)}, u32[]{:S(2)}, u32[]{:S(2)}) async-start(bf16[8,72,2048]{2,1,0:T(8,128)(2,1)} %bitcast.10), calls=%async_computation.1 | async-start | bytes 4718592 | tf_op jit(solution)/shard_map/all_to_all | solution.py:278
  127.1 28.3 %collective-permute-start.8 = (bf16[1536,384]{1,0:T(8,128)(2,1)S(1)}, bf16[1536,384]{1,0:T(8,128)(2,1)}, u32[]{:S(2)}, u32[]{:S(2)}) collective-permute-start(bf16[1536,384]{1,0:T(8,128)(2,1)S(1)} %copy-done.32), channel_id=1, source_target_pairs={{0,192},{64,0},{128,64},{192,128},{1,193},{65,1},{129,65},{193,129... | collective-permute-start | bytes 3538952 | tf_op jit(solution)/shard_map/ppermute | solution.py:21
  129.8 29.1 %collective-permute-start.9 = (bf16[1536,384]{1,0:T(8,128)(2,1)S(1)}, bf16[1536,384]{1,0:T(8,128)(2,1)}, u32[]{:S(2)}, u32[]{:S(2)}) collective-permute-start(bf16[1536,384]{1,0:T(8,128)(2,1)S(1)} %copy-done.30), channel_id=1, source_target_pairs={{0,64},{64,128},{128,192},{192,0},{1,65},{65,129},{129,193},{193,1... | collective-permute-start | bytes 3538952 | tf_op jit(solution)/shard_map/ppermute | solution.py:21
  129.8 2.2 copy-start.2
  137.1 1.6 copy-start.27
  158.9 5.8 %copy-start.34 = (bf16[1280,384]{1,0:T(8,128)(2,1)S(1)}, bf16[1280,384]{1,0:T(8,128)(2,1)}, u32[]{:S(2)}) copy-start(bf16[1280,384]{1,0:T(8,128)(2,1)} %copy-done.33) | copy-start | bytes 2949124
  158.9 5.8 %copy-start.39 = (bf16[1280,384]{1,0:T(8,128)(2,1)S(1)}, bf16[1280,384]{1,0:T(8,128)(2,1)}, u32[]{:S(2)}) copy-start(bf16[1280,384]{1,0:T(8,128)(2,1)} %copy-done.38) | copy-start | bytes 2949124
  158.9 31.9 %all-to-all-start.2 = ((bf16[8,72,2048]{2,1,0:T(8,128)(2,1)}), bf16[8,72,2048]{2,1,0:T(8,128)(2,1)}, u32[]{:S(2)}, u32[]{:S(2)}) async-start(bf16[8,72,2048]{2,1,0:T(8,128)(2,1)} %bitcast.13), calls=%async_computation.2 | async-start | bytes 4718592 | tf_op jit(solution)/shard_map/all_to_all | solution.py:278
  163.8 10.5 %copy-start.35 = (bf16[1280,384]{1,0:T(8,128)(2,1)S(1)}, bf16[1280,384]{1,0:T(8,128)(2,1)}, u32[]{:S(2)}) copy-start(bf16[1280,384]{1,0:T(8,128)(2,1)} %copy-done.33) | copy-start | bytes 2949124
  163.9 55.1 %collective-permute-start.10 = (bf16[576,2048]{1,0:T(8,128)(2,1)}, bf16[576,2048]{1,0:T(8,128)(2,1)}, u32[]{:S(2)}, u32[]{:S(2)}) collective-permute-start(bf16[576,2048]{1,0:T(8,128)(2,1)} %bitcast.9.rows_ref), channel_id=1, source_target_pairs={{0,128},{64,192},{128,0},{192,64},{1,129},{65,193},{129,1},{193,65... | collective-permute-start | bytes 7077896 | tf_op jit(solution)/shard_map/ppermute | solution.py:21
  174.4 10.1 %copy-start.4 = (bf16[1,384,4096]{2,1,0:T(8,128)(2,1)S(1)}, bf16[1,384,4096]{2,1,0:T(8,128)(2,1)}, u32[]{:S(2)}) copy-start(bf16[1,384,4096]{2,1,0:T(8,128)(2,1)} %param.13) | copy-start | bytes 9437188
  174.4 10.1 %copy-start.6 = (bf16[192,4096]{1,0:T(8,128)(2,1)S(1)}, bf16[192,4096]{1,0:T(8,128)(2,1)}, u32[]{:S(2)}) copy-start(bf16[192,4096]{1,0:T(8,128)(2,1)} %copy-done.5) | copy-start | bytes 4718596
  174.4 10.1 %copy-start.10 = (bf16[192,4096]{1,0:T(8,128)(2,1)S(1)}, bf16[192,4096]{1,0:T(8,128)(2,1)}, u32[]{:S(2)}) copy-start(bf16[192,4096]{1,0:T(8,128)(2,1)} %copy-done.9) | copy-start | bytes 4718596
  188.1 1.6 copy-start.13
  190.8 46.1 %all-to-all-start.3 = ((bf16[8,72,2560]{2,1,0:T(8,128)(2,1)}), bf16[8,72,2560]{2,1,0:T(8,128)(2,1)}, u32[]{:S(2)}, u32[]{:S(2)}) async-start(bf16[8,72,2560]{2,1,0:T(8,128)(2,1)} %bitcast.28), calls=%async_computation.3 | async-start | bytes 5898240 | tf_op jit(solution)/shard_map/all_to_all | solution.py:278
  198.3 93.6 %reduce-scatter.4.cloned.1.call-start = ((), (), s32[]{:S(2)}) async-start(), calls=%async_computation.11 | async-start | bytes 2949120 | tf_op jit(solution)/shard_map/reduce_scatter | solution.py:345
  198.3 1.2 copy-start.36
  199.5 1.2 copy-start.40
  200.7 18.3 %copy-start.37 = (bf16[1280,384]{1,0:T(8,128)(2,1)S(1)}, bf16[1280,384]{1,0:T(8,128)(2,1)}, u32[]{:S(2)}) copy-start(bf16[1280,384]{1,0:T(8,128)(2,1)} %copy-done.33) | copy-start | bytes 2949124
  210.5 17.7 %copy-start.7 = (bf16[192,4096]{1,0:T(8,128)(2,1)S(1)}, bf16[192,4096]{1,0:T(8,128)(2,1)}, u32[]{:S(2)}) copy-start(bf16[192,4096]{1,0:T(8,128)(2,1)} %copy-done.5) | copy-start | bytes 4718596
  210.5 17.7 %copy-start.11 = (bf16[192,4096]{1,0:T(8,128)(2,1)S(1)}, bf16[192,4096]{1,0:T(8,128)(2,1)}, u32[]{:S(2)}) copy-start(bf16[192,4096]{1,0:T(8,128)(2,1)} %copy-done.9) | copy-start | bytes 4718596
  230.5 1.2 copy-start.28
  235.3 1.6 copy-start.14
  236.9 1.1 copy-start.19
  243.0 1.6 copy-start.16
  244.6 38.1 %all-to-all-start.4 = ((bf16[8,72,2560]{2,1,0:T(8,128)(2,1)}), bf16[8,72,2560]{2,1,0:T(8,128)(2,1)}, u32[]{:S(2)}, u32[]{:S(2)}) async-start(bf16[8,72,2560]{2,1,0:T(8,128)(2,1)} %bitcast.29), calls=%async_computation.5 | async-start | bytes 5898240 | tf_op jit(solution)/shard_map/all_to_all | solution.py:278
  249.4 84.3 %reduce-scatter.6.cloned.1.call-start = ((), (), s32[]{:S(2)}) async-start(), calls=%async_computation.12 | async-start | bytes 2949120 | tf_op jit(solution)/shard_map/reduce_scatter | solution.py:348
  249.4 42.5 %collective-permute-start.11 = (bf16[576,1536]{1,0:T(8,128)(2,1)}, bf16[576,1536]{1,0:T(8,128)(2,1)}, u32[]{:S(2)}, u32[]{:S(2)}) collective-permute-start(bf16[576,1536]{1,0:T(8,128)(2,1)} %copy-done.28), channel_id=1, source_target_pairs={{0,128},{64,192},{128,0},{192,64},{1,129},{65,193},{129,1},{193,65... | collective-permute-start | bytes 5308424 | tf_op jit(solution)/shard_map/ppermute | solution.py:21
  250.3 2.2 copy-start.3
  282.7 1.1 copy-start.26
  288.9 1.5 copy-start.15
  292.0 84.0 %reduce-scatter.8.cloned.1.call-start = ((), (), s32[]{:S(2)}) async-start(), calls=%async_computation.13 | async-start | bytes 1769472 | tf_op jit(solution)/shard_map/reduce_scatter | solution.py:353
  292.0 1.4 copy-start.8
  293.4 1.4 copy-start.12
  294.8 1.2 copy-start.22
  299.6 25.8 %copy-start.20 = (bf16[512,576]{1,0:T(8,128)(2,1)S(1)}, bf16[512,576]{1,0:T(8,128)(2,1)}, u32[]{:S(2)}) copy-start(bf16[512,576]{1,0:T(8,128)(2,1)} %copy-done.18) | copy-start | bytes 1769476
  325.4 17.2 %copy-start.47 = (bf16[64,2560]{1,0:T(8,128)(2,1)S(1)}, bf16[64,2560]{1,0:T(8,128)(2,1)}, u32[]{:S(2)}) copy-start(bf16[64,2560]{1,0:T(8,128)(2,1)} %reduce-scatter.4.cloned.1.call-done) | copy-start | bytes 983044
  333.7 8.8 %collective-permute-start.12 = (bf16[64,2560]{1,0:T(8,128)(2,1)}, bf16[64,2560]{1,0:T(8,128)(2,1)S(1)}, u32[]{:S(2)}, u32[]{:S(2)}) collective-permute-start(bf16[64,2560]{1,0:T(8,128)(2,1)} %reduce-scatter.6.cloned.1.call-done), channel_id=1, source_target_pairs={{0,128},{64,192},{128,0},{192,64},{1,129},{65,193},{129,1},{193,65... | collective-permute-start | bytes 983048 | tf_op jit(solution)/shard_map/ppermute | solution.py:21
  (10 other events, 9.0 us)
Sparse Core Ops, SparseCore 0:
  19.0 57.0 all-gather.2
  95.2 40.9 all-gather.4
  244.8 41.4 reduce-scatter.3
  292.1 41.6 reduce-scatter.5
  336.1 39.8 reduce-scatter.7
where the time goes:
time: 386 us; the launch traced here: 384 us
  waiting for transfers between devices  162 us (42%)
  Pallas kernels  87.5 us (23%)
  starting transfers between devices  46 us (12%)
  local copies, waits for them, and re-layouts  45.9 us (12%)
  blocking collectives  25.8 us (7%)
  between operations  13.5 us (3%)
    ppermute x13, waiting for transfers between devices, shift(): lax.ppermute(block, axis, [(i, (i + by) % count) for i in range(count)])  84 us
    unnamed x102, local copies, waits for them, and re-layouts  41 us
    pallas_call x4, Pallas kernels, ffn(): pl.pallas_call(functools.partial(ffn_kernel, moves, has_add), grid=(6,),...  38.8 us
    reduce_scatter x1, waiting for transfers between devices, local(): lax.psum_scatter(apply(mix_own, late_back, 0, rest, tile), Z, scatter_dim...  33.4 us
    all_to_all x5, starting transfers between devices, exchange(): lax.all_to_all(parts, XC, split_axis=0, concat_axis=0, tiled=True)  27.4 us
    all_to_all x5, waiting for transfers between devices, exchange(): lax.all_to_all(parts, XC, split_axis=0, concat_axis=0, tiled=True)  27.3 us
    all_to_all x1, blocking collectives, exchange(): lax.all_to_all(parts, XC, split_axis=0, concat_axis=0, tiled=True)  25.8 us
    pallas_call x6, Pallas kernels, apply(): pl.pallas_call(apply_kernel, grid=(width // tile,), in_specs=[pl.BlockSpe...  21.8 us
  transfers between devices with their start and end apart: 23, of which 14 were waited for; matrix products, arithmetic and copies ran while one was open for 1% of the time, Pallas kernels for 21%

commit v1 on v0

--- a/solution.py
+++ b/solution.py
@@ -300,7 +300,7 @@
     def swap(parts):
         return shift(parts[0], Y, -1), shift(parts[1], Y, 1)
 
-    bounds = [0, width // 16 * 6, width // 16 * 11, width]
+    bounds = [0, width // 16 * 5, width // 16 * 11, width]
     side_2, side_1, side_0 = sides(after(w_gate, own_tokens), w_up, bounds, width // 16)
     down_low, down_high = swap(down_parts)
     side_0 = swap(after(side_0, down_low, down_high, other_tokens))

time: 386 us -> 387 us (level)
    unnamed x102 -> x96, local copies, waits for them, and re-layouts: 41 us -> 40.1 us
  transfers between devices with their start and end apart: 23 -> 23, of which waited for: 14 -> 14; matrix products, arithmetic and copies ran while one was open for 1% -> 1% of each run, Pallas kernels for 21% -> 20%
where the time goes in v1:
time: 387 us; the launch traced here: 385 us
  waiting for transfers between devices  164 us (42%)
  Pallas kernels  87.1 us (23%)
  starting transfers between devices  46.8 us (12%)
  local copies, waits for them, and re-layouts  45 us (12%)
  blocking collectives  25.8 us (7%)
  between operations  13.5 us (3%)
    ppermute x13, waiting for transfers between devices, shift(): lax.ppermute(block, axis, [(i, (i + by) % count) for i in range(count)])  84.2 us
    unnamed x96, local copies, waits for them, and re-layouts  40.1 us
    pallas_call x4, Pallas kernels, ffn(): pl.pallas_call(functools.partial(ffn_kernel, moves, has_add), grid=(6,),...  38.3 us
    reduce_scatter x1, waiting for transfers between devices, local(): lax.psum_scatter(apply(mix_own, late_back, 0, rest, tile), Z, scatter_dim...  33.4 us
    all_to_all x5, starting transfers between devices, exchange(): lax.all_to_all(parts, XC, split_axis=0, concat_axis=0, tiled=True)  29.5 us
    all_to_all x5, waiting for transfers between devices, exchange(): lax.all_to_all(parts, XC, split_axis=0, concat_axis=0, tiled=True)  28.4 us
    all_to_all x1, blocking collectives, exchange(): lax.all_to_all(parts, XC, split_axis=0, concat_axis=0, tiled=True)  25.8 us
    pallas_call x6, Pallas kernels, apply(): pl.pallas_call(apply_kernel, grid=(width // tile,), in_specs=[pl.BlockSpe...  21.8 us
  transfers between devices with their start and end apart: 23, of which 14 were waited for; matrix products, arithmetic and copies ran while one was open for 1% of the time, Pallas kernels for 20%

profile of v1, /device:TPU:4, one launch (start us, length us, event | category | flops | bytes accessed | tf_op | source)
XLA Modules:
  0.0 385.2 jit_solution(13107729857809086833)
XLA Ops:
  7.9 3.2 collective-permute-start
  11.1 3.9 %slice_bitcast_fusion = (bf16[192,4096]{1,0:T(8,128)(2,1)}, bf16[192,4096]{1,0:T(8,128)(2,1)}) fusion(bf16[1,384,4096]{2,1,0:T(8,128)(2,1)} %param.13), kind=kLoop, calls=%fused_computation | loop fusion | bytes 6291456 | tf_op jit(solution)/shard_map/slice | solution.py:295
  15.6 3.2 shard_map.73
  22.0 1.3 collective-permute-start.3
  23.3 1.9 copy-done.23
  25.2 1.9 copy-done.24
  27.1 2.4 shard_map.78
  35.4 26.1 %collective-permute-done.3 = bf16[64,2048]{1,0:T(8,128)(2,1)S(1)} collective-permute-done((bf16[64,2048]{1,0:T(8,128)(2,1)S(1)}, bf16[64,2048]{1,0:T(8,128)(2,1)S(1)}, u32[]{:S(2)}, u32[]{:S(2)}) %collective-permute-start.3) | collective-permute-done | bytes 262176 | tf_op jit(solution)/shard_map/ppermute | solution.py:21
  61.5 1.1 collective-permute-done.2.high_ref
  63.5 1.2 collective-permute-start.5
  64.7 11.4 %all-gather.3.cloned.1.call-done.extra_ref.value_ref = bf16[512,4224]{1,0:T(8,128)(2,1)} async-done(((bf16[64,4224]{1,0:T(8,128)(2,1)}), bf16[512,4224]{1,0:T(8,128)(2,1)}) %all-gather.3.cloned.1.call-update) | async-done | bytes 4325392 | tf_op jit(solution)/shard_map/all_gather | solution.py:310
  76.1 2.2 copy-done
  78.3 1.8 shard_map.74.matrix_ref
  80.5 2.3 shard_map.75
  82.8 1.5 copy-done.17
  84.3 3.4 shard_map.76
  87.7 4.9 %all-to-all-start = ((bf16[8,72,2048]{2,1,0:T(8,128)(2,1)}), bf16[8,72,2048]{2,1,0:T(8,128)(2,1)}, u32[]{:S(2)}, u32[]{:S(2)}) async-start(bf16[8,72,2048]{2,1,0:T(8,128)(2,1)} %bitcast.30), calls=%async_computation | async-start | bytes 4718592 | tf_op jit(solution)/shard_map/all_to_all | solution.py:278
  93.4 2.8 collective-permute-start.6
  96.2 25.5 %collective-permute-done.6.refs_2_ = bf16[1536,384]{1,0:T(8,128)(2,1)S(1)} collective-permute-done((bf16[1536,384]{1,0:T(8,128)(2,1)S(1)}, bf16[1536,384]{1,0:T(8,128)(2,1)S(1)}, u32[]{:S(2)}, u32[]{:S(2)}) %collective-permute-start.6) | collective-permute-done | bytes 1179680 | tf_op jit(solution)/shard_map/ppermute | solution.py:21
  122.8 2.4 collective-permute-done.7.refs_3_
  125.3 4.9 %all-to-all-start.1 = ((bf16[8,72,2048]{2,1,0:T(8,128)(2,1)}), bf16[8,72,2048]{2,1,0:T(8,128)(2,1)}, u32[]{:S(2)}, u32[]{:S(2)}) async-start(bf16[8,72,2048]{2,1,0:T(8,128)(2,1)} %bitcast.10), calls=%async_computation.1 | async-start | bytes 4718592 | tf_op jit(solution)/shard_map/all_to_all | solution.py:278
  130.2 1.3 collective-permute-start.8
  132.2 2.2 copy-done.2
  134.5 2.3 shard_map.77.matrix_ref
  137.6 1.8 shard_map.82.matrix_ref
  139.5 1.6 copy-done.27
  141.1 3.3 shard_map.83
  144.4 9.6 %collective-permute-done.8.refs_0_ = bf16[1280,384]{1,0:T(8,128)(2,1)S(1)} collective-permute-done((bf16[1280,384]{1,0:T(8,128)(2,1)S(1)}, bf16[1280,384]{1,0:T(8,128)(2,1)S(1)}, u32[]{:S(2)}, u32[]{:S(2)}) %collective-permute-start.8) | collective-permute-done | bytes 983072 | tf_op jit(solution)/shard_map/ppermute | solution.py:21
  154.0 2.3 collective-permute-done.9.refs_1_
  157.2 7.4 %all-to-all-start.2 = ((bf16[8,72,2048]{2,1,0:T(8,128)(2,1)}), bf16[8,72,2048]{2,1,0:T(8,128)(2,1)}, u32[]{:S(2)}, u32[]{:S(2)}) async-start(bf16[8,72,2048]{2,1,0:T(8,128)(2,1)} %bitcast.13), calls=%async_computation.2 | async-start | bytes 4718592 | tf_op jit(solution)/shard_map/all_to_all | solution.py:278
  165.0 9.5 %shard_map.79.refs_6_ = f32[576,1536]{1,0:T(8,128)} custom-call(bf16[576,2048]{1,0:T(8,128)(2,1)} %bitcast.9.rows_ref, bf16[4096,384]{1,0:T(8,128)(2,1)} %bitcast.33, bf16[4096,384]{1,0:T(8,128)(2,1)} %bitcast.38, bf16[1280,384]{1,0:T(8,128)(2,1)S(1)} %collective-permute-done.8.refs_0_, bf16[1280,384]{1,0:T(8,128)(2,1)} %collective-permute-done.9.refs_1_, ...), custom_call_target="tpu_custom_call" | custom-call | flops 5435817984 | bytes 4718592 | tf_op jit(solution)/shard_map/pallas_call | solution.py:223
  174.5 1.2 copy-done.38
  175.7 9.9 %shard_map.80.hidden_ref = bf16[576,768]{1,0:T(8,128)(2,1)S(1)} custom-call(bf16[576,2048]{1,0:T(8,128)(2,1)} %bitcast.11.rows_ref, bf16[4096,384]{1,0:T(8,128)(2,1)} %bitcast.34, bf16[4096,384]{1,0:T(8,128)(2,1)} %bitcast.39, bf16[1280,384]{1,0:T(8,128)(2,1)S(1)} %copy-done.38, bf16[1280,384]{1,0:T(8,128)(2,1)} %collective-permute-done.9.refs_1_, ...), custom_call_target="tpu_custom_call" | custom-call | flops 5435817984 | bytes 4718592 | tf_op jit(solution)/shard_map/pallas_call | solution.py:223
  185.6 3.6 shard_map.81
  189.2 1.6 copy-done.13
  191.7 7.4 %all-to-all-start.3 = ((bf16[8,72,2560]{2,1,0:T(8,128)(2,1)}), bf16[8,72,2560]{2,1,0:T(8,128)(2,1)}, u32[]{:S(2)}, u32[]{:S(2)}) async-start(bf16[8,72,2560]{2,1,0:T(8,128)(2,1)} %bitcast.28), calls=%async_computation.3 | async-start | bytes 5898240 | tf_op jit(solution)/shard_map/all_to_all | solution.py:278
  199.1 1.2 copy-done.39
  200.3 9.8 %shard_map.84.refs_6_ = f32[576,1536]{1,0:T(8,128)} custom-call(bf16[576,2048]{1,0:T(8,128)(2,1)} %bitcast.14.rows_ref, bf16[4096,384]{1,0:T(8,128)(2,1)} %bitcast.35, bf16[4096,384]{1,0:T(8,128)(2,1)} %bitcast.40, bf16[1280,384]{1,0:T(8,128)(2,1)S(1)} %copy-done.39, bf16[1280,384]{1,0:T(8,128)(2,1)} %collective-permute-done.9.refs_1_, ...), custom_call_target="tpu_custom_call" | custom-call | flops 5435817984 | bytes 4718592 | tf_op jit(solution)/shard_map/pallas_call | solution.py:223
  210.1 9.7 %collective-permute-done.10.rows_ref = bf16[576,2048]{1,0:T(8,128)(2,1)} collective-permute-done((bf16[576,2048]{1,0:T(8,128)(2,1)}, bf16[576,2048]{1,0:T(8,128)(2,1)}, u32[]{:S(2)}, u32[]{:S(2)}) %collective-permute-start.10) | collective-permute-done | bytes 2359328 | tf_op jit(solution)/shard_map/ppermute | solution.py:21
  219.7 9.2 %shard_map.85.hidden_ref = bf16[576,768]{1,0:T(8,128)(2,1)S(1)} custom-call(bf16[576,2048]{1,0:T(8,128)(2,1)} %collective-permute-done.10.rows_ref, bf16[4096,384]{1,0:T(8,128)(2,1)} %bitcast.36, bf16[4096,384]{1,0:T(8,128)(2,1)} %bitcast.41, bf16[1280,384]{1,0:T(8,128)(2,1)S(1)} %copy-done.40, bf16[1280,384]{1,0:T(8,128)(2,1)} %collective-permute-done.9.refs_1_, ...), custom_call_target="tpu_custom_call" | custom-call | flops 5435817984 | bytes 4718592 | tf_op jit(solution)/shard_map/pallas_call | solution.py:223
  228.9 2.2 shard_map.86
  231.2 1.2 copy-done.28
  232.4 3.6 shard_map.87
  236.0 1.6 copy-done.14
  238.7 5.0 %shard_map.88 = bf16[512,2560]{1,0:T(8,128)(2,1)S(1)} custom-call(bf16[512,576]{1,0:T(8,128)(2,1)S(1)} %copy-done.19, bf16[576,2560]{1,0:T(8,128)(2,1)} %bitcast.16.value_ref), custom_call_target="tpu_custom_call" | custom-call | tf_op jit(solution)/shard_map/pallas_call | solution.py:115
  243.7 1.6 copy-done.16
  245.3 4.8 %all-to-all-start.4 = ((bf16[8,72,2560]{2,1,0:T(8,128)(2,1)}), bf16[8,72,2560]{2,1,0:T(8,128)(2,1)}, u32[]{:S(2)}, u32[]{:S(2)}) async-start(bf16[8,72,2560]{2,1,0:T(8,128)(2,1)} %bitcast.29), calls=%async_computation.5 | async-start | bytes 5898240 | tf_op jit(solution)/shard_map/all_to_all | solution.py:278
  250.5 2.2 copy-done.3
  252.7 2.3 shard_map.89.matrix_ref
  255.8 27.5 %all-to-all-done.4 = bf16[8,72,2560]{2,1,0:T(8,128)(2,1)} async-done(((bf16[8,72,2560]{2,1,0:T(8,128)(2,1)}), bf16[8,72,2560]{2,1,0:T(8,128)(2,1)}, u32[]{:S(2)}, u32[]{:S(2)}) %all-to-all-start.4) | async-done | bytes 2949152 | tf_op jit(solution)/shard_map/all_to_all | solution.py:278
  284.5 5.0 %shard_map.90 = bf16[512,2560]{1,0:T(8,128)(2,1)S(1)} custom-call(bf16[512,576]{1,0:T(8,128)(2,1)S(1)} %copy-done.26, bf16[576,2560]{1,0:T(8,128)(2,1)} %bitcast.18.value_ref), custom_call_target="tpu_custom_call" | custom-call | tf_op jit(solution)/shard_map/pallas_call | solution.py:115
  289.5 1.5 copy-done.15
  291.0 1.6 collective-permute-done.11.refs_0_
  292.7 1.4 copy-done.8
  294.1 1.4 copy-done.12
  295.5 1.2 copy-done.22
  296.7 3.6 shard_map.91
  300.3 25.8 %all_to_all.30 = bf16[8,72,1536]{2,1,0:T(8,128)(2,1)S(1)} all-to-all(bf16[8,72,1536]{2,1,0:T(8,128)(2,1)S(1)} %bitcast.32), channel_id=1, replica_groups=mesh['y'=4,'z'=8,'x'=4,'c'=2] {'x','c'}, dimensions={0} | all-to-all | bytes 3538944 | tf_op jit(solution)/shard_map/all_to_all | solution.py:278
  326.0 2.9 shard_map.92
  328.9 5.7 %reduce-scatter.6.cloned.1.call-done = bf16[64,2560]{1,0:T(8,128)(2,1)} async-done(((bf16[512,2560]{1,0:T(8,128)(2,1)}), bf16[64,2560]{1,0:T(8,128)(2,1)}) %reduce-scatter.6.cloned.1.call-update) | async-done | bytes 327696 | tf_op jit(solution)/shard_map/reduce_scatter | solution.py:348
  334.7 3.1 collective-permute-start.12
  337.7 5.7 %collective-permute-done.12 = bf16[64,2560]{1,0:T(8,128)(2,1)S(1)} collective-permute-done((bf16[64,2560]{1,0:T(8,128)(2,1)}, bf16[64,2560]{1,0:T(8,128)(2,1)S(1)}, u32[]{:S(2)}, u32[]{:S(2)}) %collective-permute-start.12) | collective-permute-done | bytes 327712 | tf_op jit(solution)/shard_map/ppermute | solution.py:21
  343.5 33.4 %reduce-scatter.8.cloned.1.call-done = bf16[64,1536]{1,0:T(8,128)(2,1)} async-done(((bf16[512,1536]{1,0:T(8,128)(2,1)}), bf16[64,1536]{1,0:T(8,128)(2,1)}) %reduce-scatter.8.cloned.1.call-update) | async-done | bytes 196624 | tf_op jit(solution)/shard_map/reduce_scatter | solution.py:353
  376.9 1.8 pad_maximum_fusion
  (110 shorter events, 21.3 us)
Async XLA Ops:
  6.5 69.6 %all-gather.3.cloned.1.call-start = ((), (), s32[]{:S(2)}) async-start(), calls=%async_computation.9 | async-start | bytes 4866048 | tf_op jit(solution)/shard_map/all_gather | solution.py:310
  7.9 7.1 %copy-start.45 = (f32[16,64]{1,0:T(8,128)}, f32[16,64]{1,0:T(8,128)S(1)}, u32[]{:S(2)}) copy-start(f32[16,64]{1,0:T(8,128)S(1)} %pad_maximum_fusion.1.own_ref) | copy-start | bytes 12292
  7.9 7.1 %collective-permute-start = (f32[16,64]{1,0:T(8,128)S(1)}, f32[16,64]{1,0:T(8,128)S(1)}, u32[]{:S(2)}, u32[]{:S(2)}) collective-permute-start(f32[16,64]{1,0:T(8,128)S(1)} %pad_maximum_fusion.1.own_ref), channel_id=1, source_target_pairs={{0,128},{64,192},{128,0},{192,64},{1,129},{65,193},{129,1},{193,65... | collective-permute-start | bytes 12296 | tf_op jit(solution)/shard_map/ppermute | solution.py:21
  18.9 42.6 %collective-permute-start.1 = (bf16[192,4096]{1,0:T(8,128)(2,1)}, bf16[192,4096]{1,0:T(8,128)(2,1)S(1)}, u32[]{:S(2)}, u32[]{:S(2)}) collective-permute-start(bf16[192,4096]{1,0:T(8,128)(2,1)} %get-tuple-element.42), channel_id=1, source_target_pairs={{0,192},{64,0},{128,64},{192,128},{1,193},{65,1},{129,65},{193,129... | collective-permute-start | bytes 4718600 | tf_op jit(solution)/shard_map/ppermute | solution.py:21
  20.0 42.6 %collective-permute-start.2 = (bf16[192,4096]{1,0:T(8,128)(2,1)}, bf16[192,4096]{1,0:T(8,128)(2,1)S(1)}, u32[]{:S(2)}, u32[]{:S(2)}) collective-permute-start(bf16[192,4096]{1,0:T(8,128)(2,1)} %get-tuple-element.43), channel_id=1, source_target_pairs={{0,64},{64,128},{128,192},{192,0},{1,65},{65,129},{129,193},{193,1... | collective-permute-start | bytes 4718600 | tf_op jit(solution)/shard_map/ppermute | solution.py:21
  22.0 39.5 %collective-permute-start.3 = (bf16[64,2048]{1,0:T(8,128)(2,1)S(1)}, bf16[64,2048]{1,0:T(8,128)(2,1)S(1)}, u32[]{:S(2)}, u32[]{:S(2)}) collective-permute-start(bf16[64,2048]{1,0:T(8,128)(2,1)S(1)} %slice.19), channel_id=1, source_target_pairs={{0,128},{64,192},{128,0},{192,64},{1,129},{65,193},{129,1},{193,65... | collective-permute-start | bytes 786440 | tf_op jit(solution)/shard_map/ppermute | solution.py:21
  23.3 1.9 copy-start.23
  25.2 1.9 copy-start.24
  29.5 1.0 copy-start.29
  30.5 1.0 copy-start.31
  34.4 1.0 copy-start.42
  61.5 18.6 %copy-start.44 = (bf16[64,2048]{1,0:T(8,128)(2,1)}, bf16[64,2048]{1,0:T(8,128)(2,1)S(1)}, u32[]{:S(2)}) copy-start(bf16[64,2048]{1,0:T(8,128)(2,1)S(1)} %collective-permute-done.3) | copy-start | bytes 786436
  61.5 18.7 %copy-start.5 = (bf16[192,4096]{1,0:T(8,128)(2,1)}, bf16[192,4096]{1,0:T(8,128)(2,1)S(1)}, u32[]{:S(2)}) copy-start(bf16[192,4096]{1,0:T(8,128)(2,1)S(1)} %collective-permute-done.1.low_ref) | copy-start | bytes 4718596
  62.7 17.5 %copy-start.9 = (bf16[192,4096]{1,0:T(8,128)(2,1)}, bf16[192,4096]{1,0:T(8,128)(2,1)S(1)}, u32[]{:S(2)}) copy-start(bf16[192,4096]{1,0:T(8,128)(2,1)S(1)} %collective-permute-done.2.high_ref) | copy-start | bytes 4718596
  62.7 25.0 %collective-permute-start.4 = (bf16[1280,384]{1,0:T(8,128)(2,1)}, bf16[1280,384]{1,0:T(8,128)(2,1)}, u32[]{:S(2)}, u32[]{:S(2)}) collective-permute-start(bf16[1280,384]{1,0:T(8,128)(2,1)} %copy-done.42), channel_id=1, source_target_pairs={{0,192},{64,0},{128,64},{192,128},{1,193},{65,1},{129,65},{193,129... | collective-permute-start | bytes 2949128 | tf_op jit(solution)/shard_map/ppermute | solution.py:21
  63.5 24.2 %collective-permute-start.5 = (bf16[1280,384]{1,0:T(8,128)(2,1)}, bf16[1280,384]{1,0:T(8,128)(2,1)}, u32[]{:S(2)}, u32[]{:S(2)}) collective-permute-start(bf16[1280,384]{1,0:T(8,128)(2,1)} %copy-done.41), channel_id=1, source_target_pairs={{0,64},{64,128},{128,192},{192,0},{1,65},{65,129},{129,193},{193,1... | collective-permute-start | bytes 2949128 | tf_op jit(solution)/shard_map/ppermute | solution.py:21
  76.1 2.2 copy-start
  78.3 2.2 copy-start.1
  82.8 1.5 copy-start.17
  87.7 5.7 %copy-start.32 = (bf16[1536,384]{1,0:T(8,128)(2,1)S(1)}, bf16[1536,384]{1,0:T(8,128)(2,1)}, u32[]{:S(2)}) copy-start(bf16[1536,384]{1,0:T(8,128)(2,1)} %copy-done.31) | copy-start | bytes 3538948
  87.7 8.5 %copy-start.30 = (bf16[1536,384]{1,0:T(8,128)(2,1)S(1)}, bf16[1536,384]{1,0:T(8,128)(2,1)}, u32[]{:S(2)}) copy-start(bf16[1536,384]{1,0:T(8,128)(2,1)} %copy-done.29) | copy-start | bytes 3538948
  87.7 37.6 %all-to-all-start = ((bf16[8,72,2048]{2,1,0:T(8,128)(2,1)}), bf16[8,72,2048]{2,1,0:T(8,128)(2,1)}, u32[]{:S(2)}, u32[]{:S(2)}) async-start(bf16[8,72,2048]{2,1,0:T(8,128)(2,1)} %bitcast.30), calls=%async_computation | async-start | bytes 4718592 | tf_op jit(solution)/shard_map/all_to_all | solution.py:278
  92.6 46.9 %all-gather.5.cloned.1.call-start = ((), (), s32[]{:S(2)}) async-start(), calls=%async_computation.10 | async-start | bytes 2359296 | tf_op jit(solution)/shard_map/all_gather | solution.py:311
  93.4 28.4 %collective-permute-start.6 = (bf16[1536,384]{1,0:T(8,128)(2,1)S(1)}, bf16[1536,384]{1,0:T(8,128)(2,1)S(1)}, u32[]{:S(2)}, u32[]{:S(2)}) collective-permute-start(bf16[1536,384]{1,0:T(8,128)(2,1)S(1)} %copy-done.32), channel_id=1, source_target_pairs={{0,192},{64,0},{128,64},{192,128},{1,193},{65,1},{129,65},{193,129... | collective-permute-start | bytes 3538952 | tf_op jit(solution)/shard_map/ppermute | solution.py:21
  96.2 29.1 %collective-permute-start.7 = (bf16[1536,384]{1,0:T(8,128)(2,1)S(1)}, bf16[1536,384]{1,0:T(8,128)(2,1)}, u32[]{:S(2)}, u32[]{:S(2)}) collective-permute-start(bf16[1536,384]{1,0:T(8,128)(2,1)S(1)} %copy-done.30), channel_id=1, source_target_pairs={{0,64},{64,128},{128,192},{192,0},{1,65},{65,129},{129,193},{193,1... | collective-permute-start | bytes 3538952 | tf_op jit(solution)/shard_map/ppermute | solution.py:21
  121.7 1.1 copy-start.47
  125.3 4.9 %copy-start.36 = (bf16[1280,384]{1,0:T(8,128)(2,1)S(1)}, bf16[1280,384]{1,0:T(8,128)(2,1)}, u32[]{:S(2)}) copy-start(bf16[1280,384]{1,0:T(8,128)(2,1)} %copy-done.35) | copy-start | bytes 2949124
  125.3 6.2 %copy-start.34 = (bf16[1280,384]{1,0:T(8,128)(2,1)S(1)}, bf16[1280,384]{1,0:T(8,128)(2,1)}, u32[]{:S(2)}) copy-start(bf16[1280,384]{1,0:T(8,128)(2,1)} %copy-done.33) | copy-start | bytes 2949124
  125.3 31.9 %all-to-all-start.1 = ((bf16[8,72,2048]{2,1,0:T(8,128)(2,1)}), bf16[8,72,2048]{2,1,0:T(8,128)(2,1)}, u32[]{:S(2)}, u32[]{:S(2)}) async-start(bf16[8,72,2048]{2,1,0:T(8,128)(2,1)} %bitcast.10), calls=%async_computation.1 | async-start | bytes 4718592 | tf_op jit(solution)/shard_map/all_to_all | solution.py:278
  130.2 23.8 %collective-permute-start.8 = (bf16[1280,384]{1,0:T(8,128)(2,1)S(1)}, bf16[1280,384]{1,0:T(8,128)(2,1)S(1)}, u32[]{:S(2)}, u32[]{:S(2)}) collective-permute-start(bf16[1280,384]{1,0:T(8,128)(2,1)S(1)} %copy-done.36), channel_id=1, source_target_pairs={{0,192},{64,0},{128,64},{192,128},{1,193},{65,1},{129,65},{193,129... | collective-permute-start | bytes 2949128 | tf_op jit(solution)/shard_map/ppermute | solution.py:21
  131.5 24.8 %collective-permute-start.9 = (bf16[1280,384]{1,0:T(8,128)(2,1)S(1)}, bf16[1280,384]{1,0:T(8,128)(2,1)}, u32[]{:S(2)}, u32[]{:S(2)}) collective-permute-start(bf16[1280,384]{1,0:T(8,128)(2,1)S(1)} %copy-done.34), channel_id=1, source_target_pairs={{0,64},{64,128},{128,192},{192,0},{1,65},{65,129},{129,193},{193,1... | collective-permute-start | bytes 2949128 | tf_op jit(solution)/shard_map/ppermute | solution.py:21
  132.2 2.2 copy-start.2
  139.5 1.6 copy-start.27
  154.0 10.9 %copy-start.37 = (bf16[1280,384]{1,0:T(8,128)(2,1)}, bf16[1280,384]{1,0:T(8,128)(2,1)S(1)}, u32[]{:S(2)}) copy-start(bf16[1280,384]{1,0:T(8,128)(2,1)S(1)} %collective-permute-done.8.refs_0_) | copy-start | bytes 2949124
  157.2 34.5 %all-to-all-start.2 = ((bf16[8,72,2048]{2,1,0:T(8,128)(2,1)}), bf16[8,72,2048]{2,1,0:T(8,128)(2,1)}, u32[]{:S(2)}, u32[]{:S(2)}) async-start(bf16[8,72,2048]{2,1,0:T(8,128)(2,1)} %bitcast.13), calls=%async_computation.2 | async-start | bytes 4718592 | tf_op jit(solution)/shard_map/all_to_all | solution.py:278
  164.6 55.1 %collective-permute-start.10 = (bf16[576,2048]{1,0:T(8,128)(2,1)}, bf16[576,2048]{1,0:T(8,128)(2,1)}, u32[]{:S(2)}, u32[]{:S(2)}) collective-permute-start(bf16[576,2048]{1,0:T(8,128)(2,1)} %bitcast.9.rows_ref), channel_id=1, source_target_pairs={{0,128},{64,192},{128,0},{192,64},{1,129},{65,193},{129,1},{193,65... | collective-permute-start | bytes 7077896 | tf_op jit(solution)/shard_map/ppermute | solution.py:21
  174.5 1.2 copy-start.38
  175.7 9.9 %copy-start.4 = (bf16[1,384,4096]{2,1,0:T(8,128)(2,1)S(1)}, bf16[1,384,4096]{2,1,0:T(8,128)(2,1)}, u32[]{:S(2)}) copy-start(bf16[1,384,4096]{2,1,0:T(8,128)(2,1)} %param.13) | copy-start | bytes 9437188
  175.7 9.9 %copy-start.6 = (bf16[192,4096]{1,0:T(8,128)(2,1)S(1)}, bf16[192,4096]{1,0:T(8,128)(2,1)}, u32[]{:S(2)}) copy-start(bf16[192,4096]{1,0:T(8,128)(2,1)} %copy-done.5) | copy-start | bytes 4718596
  175.7 9.9 %copy-start.10 = (bf16[192,4096]{1,0:T(8,128)(2,1)S(1)}, bf16[192,4096]{1,0:T(8,128)(2,1)}, u32[]{:S(2)}) copy-start(bf16[192,4096]{1,0:T(8,128)(2,1)} %copy-done.9) | copy-start | bytes 4718596
  189.2 1.6 copy-start.13
  191.7 45.9 %all-to-all-start.3 = ((bf16[8,72,2560]{2,1,0:T(8,128)(2,1)}), bf16[8,72,2560]{2,1,0:T(8,128)(2,1)}, u32[]{:S(2)}, u32[]{:S(2)}) async-start(bf16[8,72,2560]{2,1,0:T(8,128)(2,1)} %bitcast.28), calls=%async_computation.3 | async-start | bytes 5898240 | tf_op jit(solution)/shard_map/all_to_all | solution.py:278
  199.1 93.5 %reduce-scatter.4.cloned.1.call-start = ((), (), s32[]{:S(2)}) async-start(), calls=%async_computation.11 | async-start | bytes 2949120 | tf_op jit(solution)/shard_map/reduce_scatter | solution.py:345
  199.1 1.2 copy-start.39
  200.3 19.5 %copy-start.40 = (bf16[1280,384]{1,0:T(8,128)(2,1)S(1)}, bf16[1280,384]{1,0:T(8,128)(2,1)}, u32[]{:S(2)}) copy-start(bf16[1280,384]{1,0:T(8,128)(2,1)} %copy-done.37) | copy-start | bytes 2949124
  210.0 18.9 %copy-start.7 = (bf16[192,4096]{1,0:T(8,128)(2,1)S(1)}, bf16[192,4096]{1,0:T(8,128)(2,1)}, u32[]{:S(2)}) copy-start(bf16[192,4096]{1,0:T(8,128)(2,1)} %copy-done.5) | copy-start | bytes 4718596
  210.1 18.9 %copy-start.11 = (bf16[192,4096]{1,0:T(8,128)(2,1)S(1)}, bf16[192,4096]{1,0:T(8,128)(2,1)}, u32[]{:S(2)}) copy-start(bf16[192,4096]{1,0:T(8,128)(2,1)} %copy-done.9) | copy-start | bytes 4718596
  231.1 1.2 copy-start.28
  236.0 1.6 copy-start.14
  237.6 1.1 copy-start.19
  243.7 1.6 copy-start.16
  245.3 38.1 %all-to-all-start.4 = ((bf16[8,72,2560]{2,1,0:T(8,128)(2,1)}), bf16[8,72,2560]{2,1,0:T(8,128)(2,1)}, u32[]{:S(2)}, u32[]{:S(2)}) async-start(bf16[8,72,2560]{2,1,0:T(8,128)(2,1)} %bitcast.29), calls=%async_computation.5 | async-start | bytes 5898240 | tf_op jit(solution)/shard_map/all_to_all | solution.py:278
  250.1 84.5 %reduce-scatter.6.cloned.1.call-start = ((), (), s32[]{:S(2)}) async-start(), calls=%async_computation.12 | async-start | bytes 2949120 | tf_op jit(solution)/shard_map/reduce_scatter | solution.py:348
  250.1 42.5 %collective-permute-start.11 = (bf16[576,1536]{1,0:T(8,128)(2,1)}, bf16[576,1536]{1,0:T(8,128)(2,1)}, u32[]{:S(2)}, u32[]{:S(2)}) collective-permute-start(bf16[576,1536]{1,0:T(8,128)(2,1)} %copy-done.28), channel_id=1, source_target_pairs={{0,128},{64,192},{128,0},{192,64},{1,129},{65,193},{129,1},{193,65... | collective-permute-start | bytes 5308424 | tf_op jit(solution)/shard_map/ppermute | solution.py:21
  250.5 2.2 copy-start.3
  283.4 1.1 copy-start.26
  289.5 1.5 copy-start.15
  292.6 84.3 %reduce-scatter.8.cloned.1.call-start = ((), (), s32[]{:S(2)}) async-start(), calls=%async_computation.13 | async-start | bytes 1769472 | tf_op jit(solution)/shard_map/reduce_scatter | solution.py:353
  292.7 1.4 copy-start.8
  294.1 1.4 copy-start.12
  295.5 1.2 copy-start.22
  300.3 25.8 %copy-start.20 = (bf16[512,576]{1,0:T(8,128)(2,1)S(1)}, bf16[512,576]{1,0:T(8,128)(2,1)}, u32[]{:S(2)}) copy-start(bf16[512,576]{1,0:T(8,128)(2,1)} %copy-done.18) | copy-start | bytes 1769476
  326.0 17.4 %copy-start.43 = (bf16[64,2560]{1,0:T(8,128)(2,1)S(1)}, bf16[64,2560]{1,0:T(8,128)(2,1)}, u32[]{:S(2)}) copy-start(bf16[64,2560]{1,0:T(8,128)(2,1)} %reduce-scatter.4.cloned.1.call-done) | copy-start | bytes 983044
  334.7 8.8 %collective-permute-start.12 = (bf16[64,2560]{1,0:T(8,128)(2,1)}, bf16[64,2560]{1,0:T(8,128)(2,1)S(1)}, u32[]{:S(2)}, u32[]{:S(2)}) collective-permute-start(bf16[64,2560]{1,0:T(8,128)(2,1)} %reduce-scatter.6.cloned.1.call-done), channel_id=1, source_target_pairs={{0,128},{64,192},{128,0},{192,64},{1,129},{65,193},{129,1},{193,65... | collective-permute-start | bytes 983048 | tf_op jit(solution)/shard_map/ppermute | solution.py:21
  (7 other events, 6.0 us)
Sparse Core Ops, SparseCore 0:
  19.0 57.0 all-gather.2
  95.3 40.9 all-gather.4
  245.4 41.9 reduce-scatter.3
  292.7 41.8 reduce-scatter.5
  337.1 39.8 reduce-scatter.7
